TPU v7x, 512 devices: a whole 4x4x16 slice. The times are simulated.
512 devices in a mesh: fsdp: 64 (over y, z), mat: 8 (over x, core).
Axes of the slice: x: 4, y: 4, z: 16, core: 2. Of those that a mesh axis runs over, the one named last changes fastest.
Arguments:
- momentum: bfloat16 [16384, 16384], P('fsdp', 'mat'), may hold values from -32 to 32
- gradient: bfloat16 [16384, 16384], P('fsdp', 'mat'), may hold values from -6 to 6
- right_factor: float32 [16384, 128], P(('mat', 'fsdp')), may hold values from -6 to 6
Outputs:
- new_momentum: bfloat16 [16384, 16384], P('fsdp', 'mat')
- update: bfloat16 [16384, 16384], P('fsdp', 'mat')
- new_right: float32 [16384, 128], P(('mat', 'fsdp'))
All inputs are finite; a program needn't handle non-finite values.
Results may differ from a plain program's by a relative error of at most 0.012.
Values may be sent and summed in bfloat16 or wider, within the bound.
A program may use at most 64 MiB of HBM per device.

v0:
```python
import math

import jax
import jax.numpy as jnp
from jax import lax
from jax.sharding import PartitionSpec as P

D = 16384
RANK = 128


keep_factor = 0.95
norm_eps = 1e-06


def partner_2(shard, axis, distance):
    return lax.ppermute(shard, axis, [(i, i ^ 1 << distance) for i in range(lax.axis_size(axis))])


def local(momentum, gradient, right_factor):
    buffer = (momentum.astype(jnp.float32) + gradient.astype(jnp.float32)).astype(jnp.bfloat16)
    right_bf = right_factor.astype(jnp.bfloat16)
    fsdp_count = lax.axis_size("fsdp")
    column_block = buffer
    partial_proj = jnp.dot(
        column_block,
        lax.all_gather(right_bf, "fsdp", axis=0, tiled=True),
        preferred_element_type=jnp.float32,
    )
    projected = lax.psum(partial_proj, "mat")
    local_gram = jnp.dot(projected.T, projected, precision=lax.Precision.HIGHEST)
    factor_low = jnp.linalg.cholesky(local_gram)
    for level_bit in range(fsdp_count.bit_length() - 1):
        partner = partner_2(factor_low, "fsdp", level_bit)
        joined = jnp.dot(factor_low, factor_low.T, precision=lax.Precision.HIGHEST)
        joined = joined + jnp.dot(partner, partner.T, precision=lax.Precision.HIGHEST)
        factor_low = jnp.linalg.cholesky(joined)
    orthonormal = lax.linalg.triangular_solve(
        factor_low, projected, left_side=False, lower=True, transpose_a=True
    )
    orth_bf = orthonormal.astype(jnp.bfloat16)
    column_block = buffer
    share_cols = lax.psum_scatter(
        lax.dot_general(
            column_block, orth_bf, (((0,), (0,)), ((), ())), preferred_element_type=jnp.float32
        ),
        "fsdp",
        scatter_dimension=0,
        tiled=True,
    )
    sumsq = lax.psum(jnp.sum(share_cols * share_cols, axis=0), ("fsdp", "mat"))
    new_right = math.sqrt(D) * share_cols * lax.rsqrt(sumsq + norm_eps)
    columns_bf, right_new_bf = (
        lax.all_gather(share_cols.astype(jnp.bfloat16), "fsdp", axis=0, tiled=True),
        lax.all_gather(new_right.astype(jnp.bfloat16), "fsdp", axis=0, tiled=True),
    )
    feedback = jnp.dot(orth_bf, columns_bf.T, preferred_element_type=jnp.float32)
    new_momentum = (buffer.astype(jnp.float32) - (1.0 - keep_factor) * feedback).astype(
        jnp.bfloat16
    )
    update = (
        math.sqrt(D / RANK) * jnp.dot(orth_bf, right_new_bf.T, preferred_element_type=jnp.float32)
    ).astype(jnp.bfloat16)
    return (new_momentum, update, new_right)


def solution(mesh):
    placed = (P("fsdp", "mat"), P("fsdp", "mat"), P(("mat", "fsdp"), None))
    return jax.shard_map(
        local,
        mesh=mesh,
        in_specs=placed,
        out_specs=(P("fsdp", "mat"), P("fsdp", "mat"), P(("mat", "fsdp"), None)),
        check_vma=False,
    )
```

profile of v0, /device:TPU:2, one launch (start us, length us, event | category | flops | bytes accessed | tf_op | source)
XLA Modules:
  0.0 1334.2 jit_solution(14288802715789185795)
XLA Ops:
  7.2 0.7 convert_element_type.34
  7.9 106.7 %all_gather.9 = bf16[2048,128]{1,0:T(8,128)(2,1)S(1)} all-gather(bf16[32,128]{1,0:T(8,128)(2,1)S(1)} %convert_element_type.34), channel_id=1, replica_groups=mesh['fsdp'=64,'mat'=8] {'fsdp'}, dimensions={0}, use_global_device_ids=true | all-gather | bytes 532480 | tf_op jit(solution)/shard_map/all_gather | solution.py:27
  114.6 2.6 fusion.25
  117.3 67.9 %all-reduce.2.cloned.1.call-done = f32[256,128]{1,0:T(8,128)} async-done(((f32[256,128]{1,0:T(8,128)}), f32[256,128]{1,0:T(8,128)}) %all-reduce.2.cloned.1.call-update) | async-done | bytes 131088 | tf_op jit(solution)/shard_map/psum | solution.py:30
  185.2 1.4 fusion.27
  186.6 11.7 cholesky.119
  198.4 0.6 compare_reduce_fusion.6
  199.0 0.7 select_select_fusion.6
  199.7 3.5 collective-permute-start
  203.2 0.3 fusion.28
  203.4 2.4 collective-permute-done
  205.9 0.3 convolution_add_fusion.5
  206.1 0.1 copy.9
  206.2 11.7 cholesky.130
  218.0 0.6 compare_reduce_fusion.5
  218.6 0.7 select_select_fusion.5
  219.3 4.6 collective-permute-start.1
  223.9 0.3 fusion.29
  224.2 2.2 collective-permute-done.1
  226.4 0.3 convolution_add_fusion.4
  226.6 0.1 copy.12
  226.7 11.7 cholesky.141
  238.5 0.6 compare_reduce_fusion.4
  239.1 0.7 select_select_fusion.4
  239.8 7.6 collective-permute-start.2
  247.4 0.3 fusion.30
  247.7 2.1 collective-permute-done.2
  249.9 0.3 convolution_add_fusion.3
  250.1 0.1 copy.15
  250.2 11.7 cholesky.152
  262.0 0.6 compare_reduce_fusion.3
  262.6 0.7 select_select_fusion.3
  263.3 15.3 %collective-permute-start.3 = (f32[128,128]{1,0:T(8,128)S(1)}, f32[128,128]{1,0:T(8,128)S(1)}, u32[]{:S(2)}, u32[]{:S(2)}) collective-permute-start(f32[128,128]{1,0:T(8,128)S(1)} %select_select_fusion.3), channel_id=1, source_target_pairs={{0,64},{8,72},{16,80},{24,88},{32,96},{40,104},{48,112},{56,120},{... | collective-permute-start | bytes 196616 | tf_op jit(solution)/shard_map/ppermute | solution.py:17
  278.6 0.3 fusion.31
  278.9 2.3 collective-permute-done.3
  281.2 0.3 convolution_add_fusion.2
  281.6 11.7 cholesky.163
  293.3 0.6 compare_reduce_fusion.2
  294.0 0.7 select_select_fusion.2
  294.7 3.4 collective-permute-start.4
  298.1 0.3 fusion.32
  298.4 2.5 collective-permute-done.4
  300.8 0.3 convolution_add_fusion.1
  301.2 11.7 cholesky.174
  313.0 0.6 compare_reduce_fusion.1
  313.6 0.7 select_select_fusion.1
  314.3 5.2 collective-permute-start.5
  319.5 0.3 fusion.33
  319.7 2.2 collective-permute-done.5
  321.9 0.3 convolution_add_fusion
  322.3 11.7 cholesky.185
  334.1 0.6 compare_reduce_fusion
  334.7 0.7 fusion.3
  335.4 9.8 custom-call.5
  345.2 0.3 convolution_convert_fusion
  345.5 1.6 fusion.24
  347.1 678.7 %reduce-scatter.2.cloned.1.call-done = f32[32,128]{1,0:T(8,128)} async-done(((f32[2048,128]{1,0:T(8,128)}), f32[32,128]{1,0:T(8,128)}) %reduce-scatter.2.cloned.1.call-update) | async-done | bytes 16400 | tf_op jit(solution)/shard_map/reduce_scatter | solution.py:43
  1025.7 0.7 multiply_reduce_fusion
  1026.5 99.9 %psum.15 = f32[128]{0:T(128)S(1)} all-reduce(f32[128]{0:T(128)S(1)} %multiply_reduce_fusion), channel_id=1, replica_groups=mesh['fsdp'=64,'mat'=8] {'fsdp','mat'}, use_global_device_ids=true, to_apply=%region_5.7 | all-reduce | flops 128 | bytes 1024 | tf_op jit(solution)/shard_map/psum | solution.py:51
  1126.4 1.4 fusion.26
  1127.8 98.8 %all_gather.11 = bf16[2048,128]{1,0:T(8,128)(2,1)S(1)} all-gather(bf16[32,128]{1,0:T(8,128)(2,1)S(1)} %get-tuple-element.4), channel_id=1, replica_groups=mesh['fsdp'=64,'mat'=8] {'fsdp'}, dimensions={0}, use_global_device_ids=true | all-gather | bytes 532480 | tf_op jit(solution)/shard_map/all_gather | solution.py:55
  1226.6 1.4 fusion.2
  1228.1 97.4 %all_gather.10 = bf16[2048,128]{1,0:T(8,128)(2,1)S(1)} all-gather(bf16[32,128]{1,0:T(8,128)(2,1)S(1)} %get-tuple-element.6), channel_id=1, replica_groups=mesh['fsdp'=64,'mat'=8] {'fsdp'}, dimensions={0}, use_global_device_ids=true | all-gather | bytes 532480 | tf_op jit(solution)/shard_map/all_gather | solution.py:54
  1325.5 1.5 fusion.1
  (29 shorter events, 0.8 us)
Async XLA Ops:
  7.2 178.0 %all-reduce.2.cloned.1.call-start = ((), (), s32[]{:S(2)}) async-start(), calls=%async_computation.1 | async-start | bytes 262144 | tf_op jit(solution)/shard_map/psum | solution.py:30
  117.3 908.5 %reduce-scatter.2.cloned.1.call-start = ((), (), s32[]{:S(2)}) async-start(), calls=%async_computation.2 | async-start | bytes 1064960 | tf_op jit(solution)/shard_map/reduce_scatter | solution.py:43
  199.7 6.2 collective-permute-start
  219.3 7.1 collective-permute-start.1
  239.8 10.1 collective-permute-start.2
  263.3 17.9 %collective-permute-start.3 = (f32[128,128]{1,0:T(8,128)S(1)}, f32[128,128]{1,0:T(8,128)S(1)}, u32[]{:S(2)}, u32[]{:S(2)}) collective-permute-start(f32[128,128]{1,0:T(8,128)S(1)} %select_select_fusion.3), channel_id=1, source_target_pairs={{0,64},{8,72},{16,80},{24,88},{32,96},{40,104},{48,112},{56,120},{... | collective-permute-start | bytes 196616 | tf_op jit(solution)/shard_map/ppermute | solution.py:17
  294.0 51.2 %copy-start.2 = (f32[256,128]{1,0:T(8,128)S(1)}, f32[256,128]{1,0:T(8,128)}, u32[]{:S(2)}) copy-start(f32[256,128]{1,0:T(8,128)} %all-reduce.2.cloned.1.call-done) | copy-start | bytes 393220
  294.7 6.2 collective-permute-start.4
  298.1 47.4 %copy-start.1 = (bf16[256,2048]{1,0:T(8,128)(2,1)S(1)}, bf16[256,2048]{1,0:T(8,128)(2,1)}, u32[]{:S(2)}) copy-start(bf16[256,2048]{1,0:T(8,128)(2,1)} %param.4) | copy-start | bytes 3145732
  298.4 47.1 %copy-start = (bf16[256,2048]{1,0:T(8,128)(2,1)S(1)}, bf16[256,2048]{1,0:T(8,128)(2,1)}, u32[]{:S(2)}) copy-start(bf16[256,2048]{1,0:T(8,128)(2,1)} %param.5) | copy-start | bytes 3145732
  314.3 7.7 collective-permute-start.5
Sparse Core Ops, SparseCore 0:
  117.4 67.7 all-reduce.1
  347.2 678.4 reduce-scatter.1
where the time goes:
time: 1340 us; the launch traced here: 1330 us
  waiting for transfers between devices  760 us (57%)
  blocking collectives  403 us (30%)
  other arithmetic  104 us (8%)
  starting transfers between devices  39.7 us (3%)
  between operations  14.8 us (1%)
    reduce_scatter x1, waiting for transfers between devices, local(): lax.psum_scatter(lax.dot_general(column_block, orth_bf, (((0,), (0,)), ((...  679 us
    all_gather x1, blocking collectives, local(): lax.all_gather(right_bf, 'fsdp', axis=0, tiled=True)  107 us
    psum x1, blocking collectives, local(): sumsq = lax.psum(jnp.sum(share_cols * share_cols, axis=0), ('fsdp', 'mat'))  99.9 us
    all_gather x1, blocking collectives, local(): lax.all_gather(new_right.astype(jnp.bfloat16), 'fsdp', axis=0, tiled=True)  98.8 us
    all_gather x1, blocking collectives, local(): lax.all_gather(share_cols.astype(jnp.bfloat16), 'fsdp', axis=0, tiled=True)  97.4 us
    another operation x18, other arithmetic, local(): factor_low = jnp.linalg.cholesky(joined)  74.3 us
    psum x1, waiting for transfers between devices, local(): projected = lax.psum(partial_proj, 'mat')  67.9 us
    ppermute x6, starting transfers between devices, partner_2(): lax.ppermute(shard, axis, [(i, i ^ 1 << distance) for i in range(lax.axis...  39.6 us
  transfers between devices with their start and end apart: 8, of which 8 were waited for; matrix products, arithmetic and copies ran while one was open for 0% of the time, Pallas kernels for 0%

commit v1 on v0

v1 whole, which is shorter than its diff:
```python
import functools
import math

import jax
import jax.numpy as jnp
from jax import lax
from jax.experimental import pallas as pl
from jax.experimental.pallas import tpu as pltpu
from jax.sharding import PartitionSpec as P

D = 16384
RANK = 128
Y, Z = 4, 16

keep_factor = 0.95
norm_eps = 1e-06

MESH = pl.DeviceIdType.MESH
F32, BF16 = jnp.float32, jnp.bfloat16
HIGH = lax.Precision.HIGHEST
BLOCK = 16


def distance(i):
    half = (i + 1) // 2
    odd = i % 2
    return half * odd + (Z - half) * (1 - odd)


def factor_inverse(a_ref, v_ref):
    n = a_ref.shape[0]
    rows = lax.broadcasted_iota(jnp.int32, (n, n), 0)
    lanes = lax.broadcasted_iota(jnp.int32, (n, n), 1)
    v_ref[...] = jnp.where(rows == lanes, 1.0, 0.0).astype(F32)
    row = lax.broadcasted_iota(jnp.int32, (BLOCK, n), 0)
    lane = lax.broadcasted_iota(jnp.int32, (BLOCK, n), 1)

    def step(j, carry):
        at = pl.ds(pl.multiple_of(j * BLOCK, BLOCK), BLOCK)
        p, v = a_ref[at, :], v_ref[at, :]
        near = pltpu.roll(p, lax.rem(n - j * BLOCK, n), 1)
        cols = [jnp.broadcast_to(near[:, k : k + 1], (BLOCK, n)) for k in range(BLOCK)]
        scale = jnp.zeros((BLOCK, n), F32)
        for k in range(BLOCK):
            pivot = cols[k][k : k + 1, :]
            root = lax.rsqrt(pivot)
            root = root * (1.5 - 0.5 * pivot * root * root)
            mult = jnp.where(row > k, cols[k] * (root * root), 0.0)
            for other in range(k + 1, BLOCK):
                cols[other] = cols[other] - mult * cols[other][k : k + 1, :]
            p = p - mult * p[k : k + 1, :]
            v = v - mult * v[k : k + 1, :]
            scale = jnp.where(row == k, root, scale)
        p, v = p * scale, v * scale
        ahead = jnp.where(lane >= (j + 1) * BLOCK, p, 0.0)
        dims = (((0,), (0,)), ((), ()))
        a_ref[...] -= lax.dot_general(ahead, p, dims, precision=HIGH, preferred_element_type=F32)
        v_ref[...] -= lax.dot_general(ahead, v, dims, precision=HIGH, preferred_element_type=F32)
        v_ref[at, :] = v
        return carry

    lax.fori_loop(0, n // BLOCK, step, 0)


def exchange(
    mom, grad, right, new_right, orth2, cg,
    mom_v, grad_v, b_v, bt_v, rg, pp, prs, pf, gp, gz, gy, gf, inv, cp, cy, cs, cz, own, sq,
    in_sem, r_zs, r_zr, r_ys, r_yr, p_s, p_r, q_s, q_r,
    gz_s, gz_r, gy_s, gy_r, gm_s, gm_r, c_ys, c_yr, c_zs, c_zr, a_zs, a_zr, a_ys, a_yr, s_s, s_r,
):
    M = prs.shape[0]
    rows, cols = b_v.shape
    chunk = cz.shape[1]
    prows = prs.shape[1]
    grows = gz.shape[1]
    f, m = lax.axis_index("fsdp"), lax.axis_index("mat")
    y, z = f // Z, f % Z

    def zpeer(d):
        return (y * Z + lax.rem(z + d, Z), m)

    def ypeer(d):
        return (lax.rem(y + d, Y) * Z + z, m)

    def mpeer(d):
        return (f, lax.rem(m + d, M))

    def part(ref, index, size):
        return ref.at[pl.ds(pl.multiple_of(index * size, size), size)]

    def copy(src, dst, send, recv, device):
        return pltpu.make_async_remote_copy(
            src_ref=src, dst_ref=dst, send_sem=send, recv_sem=recv, device_id=device, device_id_type=MESH
        )

    def loop(lo, hi, body):
        def step(i, carry):
            body(i)
            return carry

        lax.fori_loop(lo, hi, step, 0)

    load_m = pltpu.make_async_copy(mom, mom_v, in_sem.at[0])
    load_g = pltpu.make_async_copy(grad, grad_v, in_sem.at[1])
    load_m.start()
    load_g.start()
    barrier = pltpu.get_barrier_semaphore()
    loop(1, Z, lambda d: pl.semaphore_signal(barrier, 1, device_id=zpeer(d), device_id_type=MESH))
    for d in range(1, Y):
        pl.semaphore_signal(barrier, 1, device_id=ypeer(d), device_id_type=MESH)
    loop(1, M, lambda d: pl.semaphore_signal(barrier, 1, device_id=mpeer(d), device_id_type=MESH))
    part(rg, f, chunk)[...] = right[...].astype(BF16)
    load_m.wait()
    load_g.wait()
    b_v[...] = (mom_v[...].astype(F32) + grad_v[...].astype(F32)).astype(BF16)
    pl.semaphore_wait(barrier, Z - 1 + Y - 1 + M - 1)

    def gather_start(buf, zs, zr, ys, yr):
        mine = part(buf, f, chunk)

        def send(i):
            d = distance(Z - i)
            copy(mine, mine, zs.at[d], zr.at[d], zpeer(d)).start()

        loop(1, Z, send)
        for e in range(1, Y):
            copy(mine, mine, ys.at[e], yr.at[e], ypeer(e)).start()

    def gather_finish(buf, zs, zr, ys, yr):
        def onward(i):
            d = distance(i)
            block = part(buf, y * Z + lax.rem(z - d + Z, Z), chunk)
            copy(block, block, zs.at[d], zr.at[d], zpeer(d)).wait_recv()
            for e in range(1, Y):
                copy(block, block, ys.at[d * Y + e], yr.at[d * Y + e], ypeer(e)).start()

        loop(1, Z, onward)

        def arrive(i):
            d = distance(i) * jnp.minimum(i, 1)
            for e in range(1, Y):
                block = part(buf, lax.rem(y - e + Y, Y) * Z + lax.rem(z - d + Z, Z), chunk)
                copy(block, block, ys.at[d * Y + e], yr.at[d * Y + e], ypeer(e)).wait_recv()

        loop(0, Z, arrive)

    def gather_sent(buf, zs, zr, ys, yr):
        mine = part(buf, f, chunk)
        loop(1, Z, lambda d: copy(mine, mine, zs.at[d], zr.at[d], zpeer(d)).wait_send())

        def sent(d):
            block = part(buf, y * Z + lax.rem(z - d + Z, Z), chunk)
            for e in range(1, Y):
                copy(block, block, ys.at[d * Y + e], yr.at[d * Y + e], ypeer(e)).wait_send()

        loop(0, Z, sent)

    gather_start(rg, r_zs, r_zr, r_ys, r_yr)
    bt_v[...] = b_v[...].T
    gather_finish(rg, r_zs, r_zr, r_ys, r_yr)

    pp[...] = jnp.dot(b_v[...], rg[...], preferred_element_type=F32)
    loop(1, M, lambda d: copy(part(pp, lax.rem(m + d, M), prows), prs.at[d], p_s.at[d], p_r.at[d], mpeer(d)).start())
    prs[0] = part(pp, m, prows)[...]
    loop(1, M, lambda d: copy(part(pp, m, prows), prs.at[d], p_s.at[d], p_r.at[d], mpeer(d)).wait_recv())
    total = prs[0]
    for d in range(1, M):
        total = total + prs[d]
    mine = part(pf, m, prows)
    mine[...] = total
    loop(1, M, lambda d: copy(mine, mine, q_s.at[d], q_r.at[d], mpeer(d)).start())

    def whole(d):
        block = part(pf, lax.rem(m - d + M, M), prows)
        copy(block, block, q_s.at[d], q_r.at[d], mpeer(d)).wait_recv()

    loop(1, M, whole)

    p = pf[...]
    gp[...] = lax.dot_general(p, p, (((0,), (0,)), ((), ())), precision=HIGH, preferred_element_type=F32)
    gmine = part(gp, m, grows)

    def gram_send(i):
        d = distance(Z - i)
        copy(gmine, gz.at[z], gz_s.at[d], gz_r.at[d], zpeer(d)).start()

    loop(1, Z, gram_send)
    gz[z] = gmine[...]

    p1 = p.astype(BF16)
    rest = p - p1.astype(F32)
    p2 = rest.astype(BF16)
    p3 = (rest - p2.astype(F32)).astype(BF16)
    terms = jnp.concatenate([p1, p2, p3], axis=1)
    tile = 512 if cols % 512 == 0 else cols

    def product(i):
        at = pl.ds(pl.multiple_of(i * tile, tile), tile)
        out = jnp.dot(bt_v[at, :], terms, preferred_element_type=F32)
        cp[at, :] = out[:, :RANK] + out[:, RANK : 2 * RANK] + out[:, 2 * RANK :]

    loop(0, cols // tile, product)

    def target(i):
        i = Z - 1 - i
        return distance(i) * jnp.minimum(i, 1)

    def spread(i):
        d = target(i)
        to = lax.rem(z + d, Z)
        for e in range(1, Y):
            block = part(cp, lax.rem(y + e, Y) * Z + to, chunk)
            copy(block, cy.at[d * Y + e], c_ys.at[d * Y + e], c_yr.at[d * Y + e], ypeer(e)).start()

    loop(0, Z, spread)

    def combine(i):
        d = target(i)
        block = part(cp, y * Z + lax.rem(z + d, Z), chunk)
        for e in range(1, Y):
            copy(block, cy.at[d * Y + e], c_ys.at[d * Y + e], c_yr.at[d * Y + e], ypeer(e)).wait_recv()
        out = block[...]
        for e in range(1, Y):
            out = out + cy[d * Y + e]
        cs[d] = out

    def combine_send(i):
        combine(i)
        d = target(i)
        copy(cs.at[d], cz.at[d], c_zs.at[d], c_zr.at[d], zpeer(d)).start()

    loop(0, Z // 2, combine_send)

    def gram_arrive(d):
        slot = gz.at[lax.rem(z - d + Z, Z)]
        copy(gmine, slot, gz_s.at[d], gz_r.at[d], zpeer(d)).wait_recv()

    loop(1, Z, gram_arrive)
    total = gz[0]
    for k in range(1, Z):
        total = total + gz[k]
    gy[y] = total
    for e in range(1, Y):
        copy(gy.at[y], gy.at[y], gy_s.at[e], gy_r.at[e], ypeer(e)).start()

    loop(Z // 2, Z - 1, combine_send)
    combine(Z - 1)

    for e in range(1, Y):
        slot = gy.at[lax.rem(y - e + Y, Y)]
        copy(slot, slot, gy_s.at[e], gy_r.at[e], ypeer(e)).wait_recv()
    total = gy[0]
    for k in range(1, Y):
        total = total + gy[k]
    gown = part(gf, m, grows)
    gown[...] = total
    loop(1, M, lambda d: copy(gown, gown, gm_s.at[d], gm_r.at[d], mpeer(d)).start())

    def gram_whole(d):
        block = part(gf, lax.rem(m - d + M, M), grows)
        copy(block, block, gm_s.at[d], gm_r.at[d], mpeer(d)).wait_recv()

    loop(1, M, gram_whole)
    loop(1, M, lambda d: copy(gown, gown, gm_s.at[d], gm_r.at[d], mpeer(d)).wait_send())

    factor_inverse(gf, inv)
    nt = (((1,), (1,)), ((), ()))
    linv = inv[...]

    total = cs[0]
    for d in range(1, Z):
        copy(cs.at[d], cz.at[d], c_zs.at[d], c_zr.at[d], zpeer(d)).wait_recv()
        total = total + cz[d]
    columns = lax.dot_general(total, linv, nt, precision=HIGH, preferred_element_type=F32)
    own[...] = columns
    part(cg, f, chunk)[...] = columns.astype(BF16)
    gather_start(cg, a_zs, a_zr, a_ys, a_yr)
    orth = lax.dot_general(pf[...], linv, nt, precision=HIGH, preferred_element_type=F32).astype(BF16)
    orth2[pl.ds(0, rows), :] = orth
    gather_finish(cg, a_zs, a_zr, a_ys, a_yr)

    here = cg[...].astype(F32)
    sq[m] = jnp.broadcast_to(jnp.sum(here * here, axis=0, keepdims=True), sq.shape[1:])
    loop(1, M, lambda d: copy(sq.at[m], sq.at[m], s_s.at[d], s_r.at[d], mpeer(d)).start())

    def squares(d):
        slot = sq.at[lax.rem(m - d + M, M)]
        copy(slot, slot, s_s.at[d], s_r.at[d], mpeer(d)).wait_recv()

    loop(1, M, squares)
    total = sq[0]
    for k in range(1, M):
        total = total + sq[k]
    scale = math.sqrt(D) * lax.rsqrt(total[0:1, :] + norm_eps)
    new_right[...] = own[...] * scale
    orth2[pl.ds(rows, rows), :] = (orth.astype(F32) * (math.sqrt(D / RANK) * scale)).astype(BF16)

    gather_sent(rg, r_zs, r_zr, r_ys, r_yr)
    gather_sent(cg, a_zs, a_zr, a_ys, a_yr)
    loop(1, M, lambda d: copy(part(pp, m, prows), prs.at[d], p_s.at[d], p_r.at[d], mpeer(d)).wait_send())
    loop(1, M, lambda d: copy(mine, mine, q_s.at[d], q_r.at[d], mpeer(d)).wait_send())
    loop(1, Z, lambda d: copy(gmine, gz.at[z], gz_s.at[d], gz_r.at[d], zpeer(d)).wait_send())
    for e in range(1, Y):
        copy(gy.at[y], gy.at[y], gy_s.at[e], gy_r.at[e], ypeer(e)).wait_send()

    def spread_sent(d):
        for e in range(1, Y):
            copy(cs.at[d], cy.at[d * Y + e], c_ys.at[d * Y + e], c_yr.at[d * Y + e], ypeer(e)).wait_send()

    loop(0, Z, spread_sent)
    loop(1, Z, lambda d: copy(cs.at[d], cz.at[d], c_zs.at[d], c_zr.at[d], zpeer(d)).wait_send())
    loop(1, M, lambda d: copy(sq.at[m], sq.at[m], s_s.at[d], s_r.at[d], mpeer(d)).wait_send())


def finish(mom, grad, orth2, columns, new_momentum, update):
    rows = mom.shape[0]
    buffer = (mom[...].astype(F32) + grad[...].astype(F32)).astype(BF16).astype(F32)
    both = lax.dot_general(orth2[...], columns[...], (((1,), (1,)), ((), ())), preferred_element_type=F32)
    new_momentum[...] = (buffer - (1.0 - keep_factor) * both[:rows]).astype(BF16)
    update[...] = both[rows:].astype(BF16)


def local(momentum, gradient, right_factor):
    rows, cols = momentum.shape
    chunk = right_factor.shape[0]
    F, M = lax.axis_size("fsdp"), lax.axis_size("mat")
    prows, grows = rows // M, RANK // M
    vmem, dma = pltpu.VMEM, pltpu.SemaphoreType.DMA
    whole = pl.BlockSpec(memory_space=pltpu.VMEM)
    anyw = pl.BlockSpec(memory_space=pl.ANY)
    ring = [dma((Z,)), dma((Z,))]
    plane = [dma((Z * Y,)), dma((Z * Y,))]
    pair = [dma((M,)), dma((M,))]
    new_right, orth2, columns = pl.pallas_call(
        exchange,
        out_shape=(
            jax.ShapeDtypeStruct((chunk, RANK), F32),
            jax.ShapeDtypeStruct((2 * rows, RANK), BF16),
            jax.ShapeDtypeStruct((cols, RANK), BF16),
        ),
        in_specs=[anyw, anyw, whole],
        out_specs=(whole, whole, whole),
        scratch_shapes=[
            vmem((rows, cols), BF16), vmem((rows, cols), BF16), vmem((rows, cols), BF16), vmem((cols, rows), BF16),
            vmem((cols, RANK), BF16), vmem((rows, RANK), F32), vmem((M, prows, RANK), F32), vmem((rows, RANK), F32),
            vmem((RANK, RANK), F32), vmem((Z, grows, RANK), F32), vmem((Y, grows, RANK), F32),
            vmem((RANK, RANK), F32), vmem((RANK, RANK), F32),
            vmem((cols, RANK), F32), vmem((Z * Y, chunk, RANK), F32), vmem((Z, chunk, RANK), F32),
            vmem((Z, chunk, RANK), F32), vmem((chunk, RANK), F32), vmem((M, 8, RANK), F32),
            dma((2,)), *ring, *plane, *pair, *pair, *ring, dma((Y,)), dma((Y,)), *pair, *plane, *ring, *ring, *plane, *pair,
        ],
        compiler_params=pltpu.CompilerParams(
            collective_id=0, has_side_effects=True, vmem_limit_bytes=40 * 2**20
        ),
        name="exchange",
    )(momentum, gradient, right_factor)
    tile = min(512, cols)
    wide = pl.BlockSpec((rows, tile), lambda i: (0, i))
    new_momentum, update = pl.pallas_call(
        finish,
        grid=(cols // tile,),
        out_shape=(
            jax.ShapeDtypeStruct((rows, cols), BF16),
            jax.ShapeDtypeStruct((rows, cols), BF16),
        ),
        in_specs=[wide, wide, pl.BlockSpec((2 * rows, RANK), lambda i: (0, 0)), pl.BlockSpec((tile, RANK), lambda i: (i, 0))],
        out_specs=(wide, wide),
        name="finish",
    )(momentum, gradient, orth2, columns)
    return (new_momentum, update, new_right)


def solution(mesh):
    placed = (P("fsdp", "mat"), P("fsdp", "mat"), P(("mat", "fsdp"), None))
    return jax.shard_map(
        local,
        mesh=mesh,
        in_specs=placed,
        out_specs=(P("fsdp", "mat"), P("fsdp", "mat"), P(("mat", "fsdp"), None)),
        check_vma=False,
    )
```

time: 1340 us -> 103 us (0.08)
  the two profiles are of different devices: /device:TPU:2 before, /device:TPU:1 now
where the time goes in v1:
time: 103 us; the launch traced here: 102 us
  Pallas kernels  96.3 us (93%)
  local copies, waits for them, and re-layouts  5.2 us (5%)
    pallas_call x1, Pallas kernels, local(): pl.pallas_call(exchange, out_shape=(jax.ShapeDtypeStruct((chunk, RANK), F...  92 us
    unnamed x11, local copies, waits for them, and re-layouts  5.2 us
    pallas_call x1, Pallas kernels, local(): pl.pallas_call(finish, grid=(cols // tile,), out_shape=(jax.ShapeDtypeStr...  4.37 us

profile of v1, /device:TPU:1, one launch (start us, length us, event | category | flops | bytes accessed | tf_op | source)
XLA Modules:
  0.0 102.2 jit_solution(199359538198904222)
XLA Ops:
  0.6 0.0 copy-start
  0.6 1.2 %copy-done = bf16[256,2048]{1,0:T(8,128)(2,1)S(1)} copy-done((bf16[256,2048]{1,0:T(8,128)(2,1)S(1)}, bf16[256,2048]{1,0:T(8,128)(2,1)}, u32[]{:S(2)}) %copy-start) | copy-done | bytes 1048600
  1.9 0.0 copy-start.1
  1.9 1.2 %copy-done.1 = bf16[256,2048]{1,0:T(8,128)(2,1)S(1)} copy-done((bf16[256,2048]{1,0:T(8,128)(2,1)S(1)}, bf16[256,2048]{1,0:T(8,128)(2,1)}, u32[]{:S(2)}) %copy-start.1) | copy-done | bytes 1048600
  3.1 0.0 copy-start.4
  3.1 0.7 copy-done.4
  3.8 92.0 %exchange.1 = (f32[32,128]{1,0:T(8,128)S(1)}, bf16[512,128]{1,0:T(8,128)(2,1)S(1)}, bf16[2048,128]{1,0:T(8,128)(2,1)S(1)}) custom-call(bf16[256,2048]{1,0:T(8,128)(2,1)S(1)} %copy-done, bf16[256,2048]{1,0:T(8,128)(2,1)S(1)} %copy-done.1, f32[32,128]{1,0:T(8,128)S(1)} %copy-done.4), custom_call_target="tpu_custom_call" | custom-call | tf_op jit(solution)/shard_map/exchange/pallas_call | solution.py:334
  95.8 0.0 copy-start.2
  95.8 0.8 copy-done.2
  96.6 0.0 copy-start.3
  96.6 0.6 copy-done.3
  97.2 4.4 %finish.1 = (bf16[256,2048]{1,0:T(8,128)(2,1)}, bf16[256,2048]{1,0:T(8,128)(2,1)}) custom-call(bf16[256,2048]{1,0:T(8,128)(2,1)} %mom.3, bf16[256,2048]{1,0:T(8,128)(2,1)} %grad.3, bf16[512,128]{1,0:T(8,128)(2,1)} %copy-done.3, bf16[2048,128]{1,0:T(8,128)(2,1)} %copy-done.2), custom_call_target="tpu_custom_call" | custom-call | tf_op jit(solution)/shard_map/finish/pallas_call | solution.py:359
  101.6 0.6 copy.7
Async XLA Ops:
  0.6 1.2 %copy-start = (bf16[256,2048]{1,0:T(8,128)(2,1)S(1)}, bf16[256,2048]{1,0:T(8,128)(2,1)}, u32[]{:S(2)}) copy-start(bf16[256,2048]{1,0:T(8,128)(2,1)} %mom.3) | copy-start | bytes 3145732
  1.9 1.2 %copy-start.1 = (bf16[256,2048]{1,0:T(8,128)(2,1)S(1)}, bf16[256,2048]{1,0:T(8,128)(2,1)}, u32[]{:S(2)}) copy-start(bf16[256,2048]{1,0:T(8,128)(2,1)} %grad.3) | copy-start | bytes 3145732
  3.1 0.7 copy-start.4
  95.8 0.8 copy-start.2
  96.6 0.6 copy-start.3

commit v2 on v0

v2 whole, which is shorter than its diff:
```python
import functools
import math

import jax
import jax.numpy as jnp
from jax import lax
from jax.experimental import pallas as pl
from jax.experimental.pallas import tpu as pltpu
from jax.sharding import PartitionSpec as P

D = 16384
RANK = 128
Y, Z = 4, 16

keep_factor = 0.95
norm_eps = 1e-06

MESH = pl.DeviceIdType.MESH
F32, BF16 = jnp.float32, jnp.bfloat16
HIGH = lax.Precision.HIGHEST
BLOCK = 32
EARLY = 5


def factor_inverse(a_ref, v_ref):
    n = a_ref.shape[0]
    rows = lax.broadcasted_iota(jnp.int32, (n, n), 0)
    lanes = lax.broadcasted_iota(jnp.int32, (n, n), 1)
    v_ref[...] = jnp.where(rows == lanes, 1.0, 0.0).astype(F32)
    row = lax.broadcasted_iota(jnp.int32, (BLOCK, n), 0)
    lane = lax.broadcasted_iota(jnp.int32, (BLOCK, n), 1)

    def step(j, carry):
        at = pl.ds(pl.multiple_of(j * BLOCK, BLOCK), BLOCK)
        p, v = a_ref[at, :], v_ref[at, :]
        near = pltpu.roll(p, lax.rem(n - j * BLOCK, n), 1)
        cols = [jnp.broadcast_to(near[:, k : k + 1], (BLOCK, n)) for k in range(BLOCK)]
        scale = jnp.zeros((BLOCK, n), F32)
        for k in range(BLOCK):
            pivot = cols[k][k : k + 1, :]
            root = lax.rsqrt(pivot)
            root = root * (1.5 - 0.5 * pivot * root * root)
            mult = jnp.where(row > k, cols[k] * (root * root), 0.0)
            for other in range(k + 1, BLOCK):
                cols[other] = cols[other] - mult * cols[other][k : k + 1, :]
            p = p - mult * p[k : k + 1, :]
            v = v - mult * v[k : k + 1, :]
            scale = jnp.where(row == k, root, scale)
        p, v = p * scale, v * scale
        ahead = jnp.where(lane >= (j + 1) * BLOCK, p, 0.0)
        dims = (((0,), (0,)), ((), ()))
        a_ref[...] -= lax.dot_general(ahead, p, dims, precision=HIGH, preferred_element_type=F32)
        v_ref[...] -= lax.dot_general(ahead, v, dims, precision=HIGH, preferred_element_type=F32)
        v_ref[at, :] = v
        return carry

    lax.fori_loop(0, n // BLOCK, step, 0)


def exchange(
    mom, grad, right, new_right, new_momentum, update,
    mom_v, grad_v, right_v, cg, b_v, bt_v, rg, pp, prs, pf, gp, gy, gz, gf, inv, orth_v, cp, cy, cs, cz, own, sm, sy,
    in_sem, p_s, p_r, q_s, q_r, gy_s, gy_r, gz_s, gz_r, gm_s, gm_r, cy_s, cy_r, cz_s, cz_r,
    sm_s, sm_r, sy_s, sy_r, rz_s, rz_r, ry_s, ry_r, az_s, az_r, ay_s, ay_r,
):
    M = prs.shape[0]
    rows, cols = b_v.shape
    chunk = cz.shape[1]
    prows = prs.shape[1]
    grows = gz.shape[1]
    F = Y * Z
    tile = cols // Y
    ring = [d for k in range(1, Z // 2) for d in (k, Z - k)] + [Z // 2]
    nt = (((1,), (1,)), ((), ()))
    f, m = lax.axis_index("fsdp"), lax.axis_index("mat")
    y, z = f // Z, f % Z

    def zpeer(d):
        return (y * Z + lax.rem(z + d, Z), m)

    def ypeer(d):
        return (lax.rem(y + d, Y) * Z + z, m)

    def mpeer(d):
        return (f, lax.rem(m + d, M))

    def part(ref, index, size):
        return ref.at[pl.ds(pl.multiple_of(index * size, size), size)]

    def copy(src, dst, send, recv, device):
        return pltpu.make_async_remote_copy(
            src_ref=src, dst_ref=dst, send_sem=send, recv_sem=recv, device_id=device, device_id_type=MESH
        )

    def arrived(ref, sem):
        copy(ref, ref, sem, sem, zpeer(1)).wait_recv()

    pending = []

    def sent(ref, sem):
        pending.append(lambda: copy(ref, ref, sem, sem, zpeer(1)).wait_send())

    barrier = pltpu.get_barrier_semaphore()
    peers = [zpeer(d) for d in reversed(ring)] + [mpeer(d) for d in range(1, M)] + [ypeer(d) for d in range(1, Y)]
    for peer in peers:
        pl.semaphore_signal(barrier, 1, device_id=peer, device_id_type=MESH)
    load_m = pltpu.make_async_copy(mom, mom_v, in_sem.at[0])
    load_g = pltpu.make_async_copy(grad, grad_v, in_sem.at[1])
    load_r = pltpu.make_async_copy(right, right_v, in_sem.at[2])
    load_r.start()
    load_m.start()
    load_g.start()
    load_r.wait()
    part(rg, f, chunk)[...] = right_v[...].astype(BF16)
    load_m.wait()
    load_g.wait()
    b_v[...] = (mom_v[...].astype(F32) + grad_v[...].astype(F32)).astype(BF16)
    pl.semaphore_wait(barrier, len(peers))

    def block_of(buf, d):
        return part(buf, y * Z + lax.rem(z - d + Z, Z), chunk)

    def along_y(buf, d, y_s, y_r):
        block = block_of(buf, d)
        for e in (2, 1, 3):
            copy(block, block, y_s, y_r, ypeer(e)).start()

    def gather_z(buf, z_s, z_r, y_s, y_r, beside):
        mine = block_of(buf, 0)
        far = [d for d in ring if Z // 4 < d < Z - Z // 4]
        for d in reversed(far):
            copy(mine, mine, z_s, z_r.at[d], zpeer(d)).start()
        along_y(buf, 0, y_s, y_r)
        for d in ring:
            if d not in far:
                copy(mine, mine, z_s, z_r.at[d], zpeer(d)).start()
        beside()
        for d in ring:
            arrived(block_of(buf, d), z_r.at[d])
            along_y(buf, d, y_s, y_r)
        sent(buf.at[pl.ds(0, (Z - 1) * chunk)], z_s)
        sent(buf.at[pl.ds(0, (F - Z) * chunk)], y_s)

    def gather_y(buf, y_r):
        arrived(buf.at[pl.ds(0, (F - Z) * chunk)], y_r)

    def turned():
        bt_v[...] = b_v[...].T

    gather_z(rg, rz_s, rz_r, ry_s, ry_r, turned)
    gather_y(rg, ry_r)

    pp[...] = jnp.dot(b_v[...], rg[...], preferred_element_type=F32)
    for d in range(1, M):
        copy(part(pp, lax.rem(m + d, M), prows), prs.at[d], p_s, p_r, mpeer(d)).start()
    prs[0] = part(pp, m, prows)[...]
    arrived(prs.at[pl.ds(1, M - 1)], p_r)
    sent(prs.at[pl.ds(1, M - 1)], p_s)
    total = prs[0]
    for d in range(1, M):
        total = total + prs[d]
    mine = part(pf, m, prows)
    mine[...] = total
    for d in range(1, M):
        copy(mine, mine, q_s, q_r, mpeer(d)).start()
    arrived(pf.at[pl.ds(0, (M - 1) * prows)], q_r)
    sent(pf.at[pl.ds(0, (M - 1) * prows)], q_s)

    p = pf[...]
    gp[...] = lax.dot_general(p, p, (((0,), (0,)), ((), ())), precision=HIGH, preferred_element_type=F32)
    gmine = part(gp, m, grows)

    gy[y] = gmine[...]
    for e in (2, 1, 3):
        copy(gmine, gy.at[y], gy_s, gy_r, ypeer(e)).start()
    sent(gy.at[pl.ds(0, Y - 1)], gy_s)

    p1 = p.astype(BF16)
    rest = p - p1.astype(F32)
    p2 = rest.astype(BF16)
    p3 = (rest - p2.astype(F32)).astype(BF16)
    terms = jnp.concatenate([p1, p2, p3], axis=1)
    def product(i):
        at = pl.ds(pl.multiple_of(i * tile, tile), tile)
        out = jnp.dot(bt_v[at, :], terms, preferred_element_type=F32)
        cp[at, :] = out[:, :RANK] + out[:, RANK : 2 * RANK] + out[:, 2 * RANK :]

    def loop(lo, hi, body):
        def step(i, carry):
            body(i)
            return carry

        lax.fori_loop(lo, hi, step, 0)

    loop(0, Y, product)

    def term(e, d):
        return part(cp, lax.rem(y + e, Y) * Z + lax.rem(z + d, Z), chunk)

    order = [*reversed(ring), 0]
    for d in order:
        for e in (2, 1, 3):
            copy(term(e, d), cy.at[d, e - 1], cy_s, cy_r.at[d], ypeer(e)).start()
    sent(cp.at[pl.ds(0, (F - Z) * chunk)], cy_s)

    arrived(gy.at[pl.ds(0, Y - 1)], gy_r)
    total = gy[0]
    for k in range(1, Y):
        total = total + gy[k]
    gz[z] = total
    for d in reversed(ring):
        copy(gz.at[z], gz.at[z], gz_s, gz_r, zpeer(d)).start()
    sent(gz.at[pl.ds(0, Z - 1)], gz_s)

    def combine(d):
        arrived(cy.at[d], cy_r.at[d])
        cs[d] = term(0, d)[...] + cy[d, 0] + cy[d, 1] + cy[d, 2]

    def combine_send(d):
        combine(d)
        copy(cs.at[d], cz.at[d], cz_s, cz_r, zpeer(d)).start()

    for d in order[:EARLY]:
        combine_send(d)

    arrived(gz.at[pl.ds(0, Z - 1)], gz_r)
    total = gz[0]
    for k in range(1, Z):
        total = total + gz[k]
    gown = part(gf, m, grows)
    gown[...] = total
    for d in range(1, M):
        copy(gown, gown, gm_s, gm_r, mpeer(d)).start()
    for d in order[EARLY : Z - 1]:
        combine_send(d)
    combine(0)
    arrived(gf.at[pl.ds(0, (M - 1) * grows)], gm_r)
    copy(gf.at[pl.ds(0, (M - 1) * grows)], gown, gm_s, gm_s, zpeer(1)).wait_send()

    factor_inverse(gf, inv)
    sent(cz.at[pl.ds(0, Z - 1)], cz_s)
    linv = inv[...]

    arrived(cz.at[pl.ds(1, Z - 1)], cz_r)
    total = cs[0]
    for d in range(1, Z):
        total = total + cz[d]
    columns = lax.dot_general(total, linv, nt, precision=HIGH, preferred_element_type=F32)
    own[...] = columns
    part(cg, f, chunk)[...] = columns.astype(BF16)

    def turned_back():
        orth_v[...] = lax.dot_general(pf[...], linv, nt, precision=HIGH, preferred_element_type=F32).astype(BF16)

    gather_z(cg, az_s, az_r, ay_s, ay_r, turned_back)

    here = part(cg, y, tile)[...].astype(F32)
    sm[m] = jnp.sum(here * here, axis=0, keepdims=True)
    for d in range(1, M):
        copy(sm.at[m], sm.at[m], sm_s, sm_r, mpeer(d)).start()
    sent(sm.at[pl.ds(0, M - 1)], sm_s)

    def feedback(i):
        at = pl.ds(pl.multiple_of(i * tile, tile), tile)
        out = lax.dot_general(orth_v[...], cg[at, :], nt, preferred_element_type=F32)
        new_momentum[:, at] = (b_v[:, at].astype(F32) - (1.0 - keep_factor) * out).astype(BF16)

    feedback(y)
    arrived(sm.at[pl.ds(0, M - 1)], sm_r)
    total = sm[0]
    for k in range(1, M):
        total = total + sm[k]
    sy[y] = total
    for e in (2, 1, 3):
        copy(sy.at[y], sy.at[y], sy_s, sy_r, ypeer(e)).start()
    sent(sy.at[pl.ds(0, Y - 1)], sy_s)
    gather_y(cg, ay_r)
    loop(1, Y, lambda e: feedback(lax.rem(y + e, Y)))
    arrived(sy.at[pl.ds(0, Y - 1)], sy_r)
    total = sy[0]
    for k in range(1, Y):
        total = total + sy[k]
    scale = math.sqrt(D) * lax.rsqrt(total + norm_eps)
    new_right[...] = own[...] * scale
    scaled = (orth_v[...].astype(F32) * (math.sqrt(D / RANK) * scale)).astype(BF16)

    def outer(i):
        at = pl.ds(pl.multiple_of(i * tile, tile), tile)
        update[:, at] = lax.dot_general(scaled, cg[at, :], nt, preferred_element_type=F32).astype(BF16)

    loop(0, Y, outer)

    for wait in pending:
        wait()


def local(momentum, gradient, right_factor):
    rows, cols = momentum.shape
    chunk = right_factor.shape[0]
    F, M = lax.axis_size("fsdp"), lax.axis_size("mat")
    prows, grows = rows // M, RANK // M
    vmem, dma = pltpu.VMEM, pltpu.SemaphoreType.DMA
    whole = pl.BlockSpec(memory_space=pltpu.VMEM)
    hbm = pl.BlockSpec(memory_space=pltpu.HBM)
    ring = [dma((Z,)), dma((Z,))]
    plane = [dma((Z * Y,)), dma((Z * Y,))]
    pair = [dma((M,)), dma((M,))]
    new_right, new_momentum, update = pl.pallas_call(
        exchange,
        out_shape=(
            jax.ShapeDtypeStruct((chunk, RANK), F32),
            jax.ShapeDtypeStruct((rows, cols), BF16),
            jax.ShapeDtypeStruct((rows, cols), BF16),
        ),
        in_specs=[hbm, hbm, hbm],
        out_specs=(whole, whole, whole),
        scratch_shapes=[
            vmem((rows, cols), BF16), vmem((rows, cols), BF16), vmem((chunk, RANK), F32), vmem((cols, RANK), BF16),
            vmem((rows, cols), BF16), vmem((cols, rows), BF16),
            vmem((cols, RANK), BF16), vmem((rows, RANK), F32), vmem((M, prows, RANK), F32), vmem((rows, RANK), F32),
            vmem((RANK, RANK), F32), vmem((Y, grows, RANK), F32), vmem((Z, grows, RANK), F32),
            vmem((RANK, RANK), F32), vmem((RANK, RANK), F32), vmem((rows, RANK), BF16),
            vmem((cols, RANK), F32), vmem((Z, Y - 1, chunk, RANK), F32), vmem((Z, chunk, RANK), F32),
            vmem((Z, chunk, RANK), F32), vmem((chunk, RANK), F32), vmem((M, 1, RANK), F32), vmem((Y, 1, RANK), F32),
            dma((3,)), *[dma(())] * 11, dma((Z,)), *[dma(())] * 6, *[dma(()), dma((Z,)), dma(()), dma(())] * 2,
        ],
        compiler_params=pltpu.CompilerParams(
            collective_id=0, has_side_effects=True, vmem_limit_bytes=51 * 2**20
        ),
        name="exchange",
    )(momentum, gradient, right_factor)
    return (new_momentum, update, new_right)


def solution(mesh):
    placed = (P("fsdp", "mat"), P("fsdp", "mat"), P(("mat", "fsdp"), None))
    return jax.shard_map(
        local,
        mesh=mesh,
        in_specs=placed,
        out_specs=(P("fsdp", "mat"), P("fsdp", "mat"), P(("mat", "fsdp"), None)),
        check_vma=False,
    )
```

time: 1340 us -> 83.6 us (0.06)
  the two profiles are of different devices: /device:TPU:2 before, /device:TPU:1 now
where the time goes in v2:
time: 83.6 us; the launch traced here: 83.4 us
  Pallas kernels  79.5 us (95%)
  local copies, waits for them, and re-layouts  3.26 us (4%)
    pallas_call x1, Pallas kernels, local(): pl.pallas_call(exchange, out_shape=(jax.ShapeDtypeStruct((chunk, RANK), F...  79.5 us
    unnamed x5, local copies, waits for them, and re-layouts  3.26 us

profile of v2, /device:TPU:1, one launch (start us, length us, event | category | flops | bytes accessed | tf_op | source)
XLA Modules:
  0.0 83.4 jit_solution(16332906738458597761)
XLA Ops:
  0.6 0.0 copy-start
  0.6 0.7 copy-done
  1.3 79.5 %exchange.1 = (f32[32,128]{1,0:T(8,128)S(1)}, bf16[256,2048]{1,0:T(8,128)(2,1)S(1)}, bf16[256,2048]{1,0:T(8,128)(2,1)S(1)}) custom-call(bf16[256,2048]{1,0:T(8,128)(2,1)} %mom.1, bf16[256,2048]{1,0:T(8,128)(2,1)} %grad.1, f32[32,128]{1,0:T(8,128)S(1)} %copy-done), custom_call_target="tpu_custom_call" | custom-call | tf_op jit(solution)/shard_map/exchange/pallas_call | solution.py:308
  80.9 1.0 %copy.9 = bf16[256,2048]{1,0:T(8,128)(2,1)} copy(bf16[256,2048]{1,0:T(8,128)(2,1)S(1)} %get-tuple-element.12) | data formatting | bytes 2097152
  81.9 1.0 %copy.10 = bf16[256,2048]{1,0:T(8,128)(2,1)} copy(bf16[256,2048]{1,0:T(8,128)(2,1)S(1)} %get-tuple-element.13) | data formatting | bytes 2097152
  82.8 0.6 copy.11
Async XLA Ops:
  0.6 0.7 copy-start

commit v3 on v2

--- a/solution.py
+++ b/solution.py
@@ -35,7 +35,7 @@
         p, v = a_ref[at, :], v_ref[at, :]
         near = pltpu.roll(p, lax.rem(n - j * BLOCK, n), 1)
         cols = [jnp.broadcast_to(near[:, k : k + 1], (BLOCK, n)) for k in range(BLOCK)]
-        scale = jnp.zeros((BLOCK, n), F32)
+        pivots = jnp.zeros((BLOCK, n), F32)
         for k in range(BLOCK):
             pivot = cols[k][k : k + 1, :]
             root = lax.rsqrt(pivot)
@@ -45,7 +45,9 @@
                 cols[other] = cols[other] - mult * cols[other][k : k + 1, :]
             p = p - mult * p[k : k + 1, :]
             v = v - mult * v[k : k + 1, :]
-            scale = jnp.where(row == k, root, scale)
+            pivots = jnp.where(row == k, pivot, pivots)
+        scale = lax.rsqrt(pivots)
+        scale = scale * (1.5 - 0.5 * pivots * scale * scale)
         p, v = p * scale, v * scale
         ahead = jnp.where(lane >= (j + 1) * BLOCK, p, 0.0)
         dims = (((0,), (0,)), ((), ()))
@@ -59,9 +61,9 @@
 
 def exchange(
     mom, grad, right, new_right, new_momentum, update,
-    mom_v, grad_v, right_v, cg, b_v, bt_v, rg, pp, prs, pf, gp, gy, gz, gf, inv, orth_v, cp, cy, cs, cz, own, sm, sy,
+    mom_v, grad_v, right_v, cg, b_v, bt_v, rg, pp, prs, pf, gp, gy, gz, gf, inv, orth_v, cp, cy, cs, cz, own, sm, sz, sy,
     in_sem, p_s, p_r, q_s, q_r, gy_s, gy_r, gz_s, gz_r, gm_s, gm_r, cy_s, cy_r, cz_s, cz_r,
-    sm_s, sm_r, sy_s, sy_r, rz_s, rz_r, ry_s, ry_r, az_s, az_r, ay_s, ay_r,
+    sm_s, sm_r, sz_s, sz_r, sy_s, sy_r, rz_s, rz_r, ry_s, ry_r, az_s, az_r, ay_s, ay_r,
 ):
     M = prs.shape[0]
     rows, cols = b_v.shape
@@ -71,6 +73,7 @@
     F = Y * Z
     tile = cols // Y
     ring = [d for k in range(1, Z // 2) for d in (k, Z - k)] + [Z // 2]
+    mats = sorted(range(1, M), key=lambda d: abs(2 * d - M))
     nt = (((1,), (1,)), ((), ()))
     f, m = lax.axis_index("fsdp"), lax.axis_index("mat")
     y, z = f // Z, f % Z
@@ -101,7 +104,8 @@
         pending.append(lambda: copy(ref, ref, sem, sem, zpeer(1)).wait_send())
 
     barrier = pltpu.get_barrier_semaphore()
-    peers = [zpeer(d) for d in reversed(ring)] + [mpeer(d) for d in range(1, M)] + [ypeer(d) for d in range(1, Y)]
+    near = Z // 4
+    peers = [zpeer(d) for d in reversed(ring[: 2 * near])] + [mpeer(d) for d in range(1, M)] + [ypeer(d) for d in range(1, Y)]
     for peer in peers:
         pl.semaphore_signal(barrier, 1, device_id=peer, device_id_type=MESH)
     load_m = pltpu.make_async_copy(mom, mom_v, in_sem.at[0])
@@ -123,7 +127,7 @@
     def along_y(buf, d, y_s, y_r):
         block = block_of(buf, d)
         for e in (2, 1, 3):
-            copy(block, block, y_s, y_r, ypeer(e)).start()
+            copy(block, block, y_s, y_r.at[e], ypeer(e)).start()
 
     def gather_z(buf, z_s, z_r, y_s, y_r, beside):
         mine = block_of(buf, 0)
@@ -141,17 +145,50 @@
         sent(buf.at[pl.ds(0, (Z - 1) * chunk)], z_s)
         sent(buf.at[pl.ds(0, (F - Z) * chunk)], y_s)
 
-    def gather_y(buf, y_r):
-        arrived(buf.at[pl.ds(0, (F - Z) * chunk)], y_r)
+    def gather_z_relayed(buf, z_s, z_r, y_s, y_r, beside):
+        def along_z(d, k):
+            to = (d + k) % Z
+            copy(block_of(buf, d), block_of(buf, d), z_s, z_r.at[to], zpeer(k)).start()
+
+        def take(d):
+            arrived(block_of(buf, d), z_r.at[d])
+
+        for k in range(near, 0, -1):
+            along_z(0, k)
+            along_z(0, Z - k)
+        along_y(buf, 0, y_s, y_r)
+        beside()
+        first = ring[: near // 2 * 2]
+        for d in first:
+            take(d)
+            along_y(buf, d, y_s, y_r)
+        take(near)
+        for k in range(near, 0, -1):
+            along_z(near, k)
+        take(Z - near)
+        for k in range(near - 1, 0, -1):
+            along_z(Z - near, Z - k)
+        along_y(buf, near, y_s, y_r)
+        along_y(buf, Z - near, y_s, y_r)
+        for d in ring:
+            if d not in (*first, near, Z - near):
+                take(d)
+                along_y(buf, d, y_s, y_r)
+        sent(buf.at[pl.ds(0, (Z - 1) * chunk)], z_s)
+        sent(buf.at[pl.ds(0, (F - Z) * chunk)], y_s)
+
+    def gather_y(buf, y_r, e):
+        arrived(buf.at[pl.ds(0, Z * chunk)], y_r.at[e])
 
     def turned():
         bt_v[...] = b_v[...].T
 
-    gather_z(rg, rz_s, rz_r, ry_s, ry_r, turned)
-    gather_y(rg, ry_r)
-
+    gather_z_relayed(rg, rz_s, rz_r, ry_s, ry_r, turned)
+
+    for e in (1, 3, 2):
+        gather_y(rg, ry_r, e)
     pp[...] = jnp.dot(b_v[...], rg[...], preferred_element_type=F32)
-    for d in range(1, M):
+    for d in mats:
         copy(part(pp, lax.rem(m + d, M), prows), prs.at[d], p_s, p_r, mpeer(d)).start()
     prs[0] = part(pp, m, prows)[...]
     arrived(prs.at[pl.ds(1, M - 1)], p_r)
@@ -161,7 +198,7 @@
         total = total + prs[d]
     mine = part(pf, m, prows)
     mine[...] = total
-    for d in range(1, M):
+    for d in mats:
         copy(mine, mine, q_s, q_r, mpeer(d)).start()
     arrived(pf.at[pl.ds(0, (M - 1) * prows)], q_r)
     sent(pf.at[pl.ds(0, (M - 1) * prows)], q_s)
@@ -229,7 +266,7 @@
         total = total + gz[k]
     gown = part(gf, m, grows)
     gown[...] = total
-    for d in range(1, M):
+    for d in mats:
         copy(gown, gown, gm_s, gm_r, mpeer(d)).start()
     for d in order[EARLY : Z - 1]:
         combine_send(d)
@@ -249,16 +286,31 @@
     own[...] = columns
     part(cg, f, chunk)[...] = columns.astype(BF16)
 
-    def turned_back():
+    sm[m] = jnp.sum(columns * columns, axis=0, keepdims=True)
+
+    def squares():
+        for d in mats:
+            copy(sm.at[m], sm.at[m], sm_s, sm_r, mpeer(d)).start()
+        sent(sm.at[pl.ds(0, M - 1)], sm_s)
         orth_v[...] = lax.dot_general(pf[...], linv, nt, precision=HIGH, preferred_element_type=F32).astype(BF16)
-
-    gather_z(cg, az_s, az_r, ay_s, ay_r, turned_back)
-
-    here = part(cg, y, tile)[...].astype(F32)
-    sm[m] = jnp.sum(here * here, axis=0, keepdims=True)
-    for d in range(1, M):
-        copy(sm.at[m], sm.at[m], sm_s, sm_r, mpeer(d)).start()
-    sent(sm.at[pl.ds(0, M - 1)], sm_s)
+        arrived(sm.at[pl.ds(0, M - 1)], sm_r)
+        total = sm[0]
+        for k in range(1, M):
+            total = total + sm[k]
+        sz[z] = total
+        for d in reversed(ring):
+            copy(sz.at[z], sz.at[z], sz_s, sz_r, zpeer(d)).start()
+        sent(sz.at[pl.ds(0, Z - 1)], sz_s)
+
+    gather_z(cg, az_s, az_r, ay_s, ay_r, squares)
+    arrived(sz.at[pl.ds(0, Z - 1)], sz_r)
+    total = sz[0]
+    for k in range(1, Z):
+        total = total + sz[k]
+    sy[y] = total
+    for e in (2, 1, 3):
+        copy(sy.at[y], sy.at[y], sy_s, sy_r, ypeer(e)).start()
+    sent(sy.at[pl.ds(0, Y - 1)], sy_s)
 
     def feedback(i):
         at = pl.ds(pl.multiple_of(i * tile, tile), tile)
@@ -266,16 +318,9 @@
         new_momentum[:, at] = (b_v[:, at].astype(F32) - (1.0 - keep_factor) * out).astype(BF16)
 
     feedback(y)
-    arrived(sm.at[pl.ds(0, M - 1)], sm_r)
-    total = sm[0]
-    for k in range(1, M):
-        total = total + sm[k]
-    sy[y] = total
-    for e in (2, 1, 3):
-        copy(sy.at[y], sy.at[y], sy_s, sy_r, ypeer(e)).start()
-    sent(sy.at[pl.ds(0, Y - 1)], sy_s)
-    gather_y(cg, ay_r)
-    loop(1, Y, lambda e: feedback(lax.rem(y + e, Y)))
+    for e in (1, 3, 2):
+        gather_y(cg, ay_r, e)
+        feedback(lax.rem(y - e + Y, Y))
     arrived(sy.at[pl.ds(0, Y - 1)], sy_r)
     total = sy[0]
     for k in range(1, Y):
@@ -321,8 +366,9 @@
             vmem((RANK, RANK), F32), vmem((Y, grows, RANK), F32), vmem((Z, grows, RANK), F32),
             vmem((RANK, RANK), F32), vmem((RANK, RANK), F32), vmem((rows, RANK), BF16),
             vmem((cols, RANK), F32), vmem((Z, Y - 1, chunk, RANK), F32), vmem((Z, chunk, RANK), F32),
-            vmem((Z, chunk, RANK), F32), vmem((chunk, RANK), F32), vmem((M, 1, RANK), F32), vmem((Y, 1, RANK), F32),
-            dma((3,)), *[dma(())] * 11, dma((Z,)), *[dma(())] * 6, *[dma(()), dma((Z,)), dma(()), dma(())] * 2,
+            vmem((Z, chunk, RANK), F32), vmem((chunk, RANK), F32), vmem((M, 1, RANK), F32), vmem((Z, 1, RANK), F32),
+            vmem((Y, 1, RANK), F32),
+            dma((3,)), *[dma(())] * 11, dma((Z,)), *[dma(())] * 8, *[dma(()), dma((Z,)), dma(()), dma((Y,))] * 2,
         ],
         compiler_params=pltpu.CompilerParams(
             collective_id=0, has_side_effects=True, vmem_limit_bytes=51 * 2**20

time: 83.6 us -> 78.3 us (0.937)
  Pallas kernels: 79.5 us -> 74.1 us
    pallas_call x1, Pallas kernels: 79.5 us -> 74.1 us  [local(): pl.pallas_call(exchange, out_shape=(jax.ShapeDtypeStruct((chunk, RANK), F...]
where the time goes in v3:
time: 78.3 us; the launch traced here: 78 us
  Pallas kernels  74.1 us (95%)
  local copies, waits for them, and re-layouts  3.26 us (4%)
    pallas_call x1, Pallas kernels, local(): pl.pallas_call(exchange, out_shape=(jax.ShapeDtypeStruct((chunk, RANK), F...  74.1 us
    unnamed x5, local copies, waits for them, and re-layouts  3.26 us

profile of v3, /device:TPU:1, one launch (start us, length us, event | category | flops | bytes accessed | tf_op | source)
XLA Modules:
  0.0 78.0 jit_solution(17954830906903925725)
XLA Ops:
  0.6 0.0 copy-start
  0.6 0.7 copy-done
  1.3 74.1 %exchange.1 = (f32[32,128]{1,0:T(8,128)S(1)}, bf16[256,2048]{1,0:T(8,128)(2,1)S(1)}, bf16[256,2048]{1,0:T(8,128)(2,1)S(1)}) custom-call(bf16[256,2048]{1,0:T(8,128)(2,1)} %mom.1, bf16[256,2048]{1,0:T(8,128)(2,1)} %grad.1, f32[32,128]{1,0:T(8,128)S(1)} %copy-done), custom_call_target="tpu_custom_call" | custom-call | tf_op jit(solution)/shard_map/exchange/pallas_call | solution.py:353
  75.5 1.0 %copy.9 = bf16[256,2048]{1,0:T(8,128)(2,1)} copy(bf16[256,2048]{1,0:T(8,128)(2,1)S(1)} %get-tuple-element.12) | data formatting | bytes 2097152
  76.5 1.0 %copy.10 = bf16[256,2048]{1,0:T(8,128)(2,1)} copy(bf16[256,2048]{1,0:T(8,128)(2,1)S(1)} %get-tuple-element.13) | data formatting | bytes 2097152
  77.4 0.6 copy.11
Async XLA Ops:
  0.6 0.7 copy-start

commit v4 on v3

--- a/solution.py
+++ b/solution.py
@@ -130,22 +130,6 @@
             copy(block, block, y_s, y_r.at[e], ypeer(e)).start()
 
     def gather_z(buf, z_s, z_r, y_s, y_r, beside):
-        mine = block_of(buf, 0)
-        far = [d for d in ring if Z // 4 < d < Z - Z // 4]
-        for d in reversed(far):
-            copy(mine, mine, z_s, z_r.at[d], zpeer(d)).start()
-        along_y(buf, 0, y_s, y_r)
-        for d in ring:
-            if d not in far:
-                copy(mine, mine, z_s, z_r.at[d], zpeer(d)).start()
-        beside()
-        for d in ring:
-            arrived(block_of(buf, d), z_r.at[d])
-            along_y(buf, d, y_s, y_r)
-        sent(buf.at[pl.ds(0, (Z - 1) * chunk)], z_s)
-        sent(buf.at[pl.ds(0, (F - Z) * chunk)], y_s)
-
-    def gather_z_relayed(buf, z_s, z_r, y_s, y_r, beside):
         def along_z(d, k):
             to = (d + k) % Z
             copy(block_of(buf, d), block_of(buf, d), z_s, z_r.at[to], zpeer(k)).start()
@@ -183,7 +167,7 @@
     def turned():
         bt_v[...] = b_v[...].T
 
-    gather_z_relayed(rg, rz_s, rz_r, ry_s, ry_r, turned)
+    gather_z(rg, rz_s, rz_r, ry_s, ry_r, turned)
 
     for e in (1, 3, 2):
         gather_y(rg, ry_r, e)

time: 78.3 us -> 77.2 us (0.986)
  Pallas kernels: 74.1 us -> 73.1 us
    pallas_call x1, Pallas kernels: 74.1 us -> 73.1 us  [local(): pl.pallas_call(exchange, out_shape=(jax.ShapeDtypeStruct((chunk, RANK), F...]
where the time goes in v4:
time: 77.2 us; the launch traced here: 77 us
  Pallas kernels  73.1 us (95%)
  local copies, waits for them, and re-layouts  3.26 us (4%)
    pallas_call x1, Pallas kernels, local(): pl.pallas_call(exchange, out_shape=(jax.ShapeDtypeStruct((chunk, RANK), F...  73.1 us
    unnamed x5, local copies, waits for them, and re-layouts  3.26 us

profile of v4, /device:TPU:1, one launch (start us, length us, event | category | flops | bytes accessed | tf_op | source)
XLA Modules:
  0.0 77.0 jit_solution(1552674482909547207)
XLA Ops:
  0.6 0.0 copy-start
  0.6 0.7 copy-done
  1.3 73.1 %exchange.1 = (f32[32,128]{1,0:T(8,128)S(1)}, bf16[256,2048]{1,0:T(8,128)(2,1)S(1)}, bf16[256,2048]{1,0:T(8,128)(2,1)S(1)}) custom-call(bf16[256,2048]{1,0:T(8,128)(2,1)} %mom.1, bf16[256,2048]{1,0:T(8,128)(2,1)} %grad.1, f32[32,128]{1,0:T(8,128)S(1)} %copy-done), custom_call_target="tpu_custom_call" | custom-call | tf_op jit(solution)/shard_map/exchange/pallas_call | solution.py:337
  74.5 1.0 %copy.9 = bf16[256,2048]{1,0:T(8,128)(2,1)} copy(bf16[256,2048]{1,0:T(8,128)(2,1)S(1)} %get-tuple-element.12) | data formatting | bytes 2097152
  75.5 1.0 %copy.10 = bf16[256,2048]{1,0:T(8,128)(2,1)} copy(bf16[256,2048]{1,0:T(8,128)(2,1)S(1)} %get-tuple-element.13) | data formatting | bytes 2097152
  76.4 0.6 copy.11
Async XLA Ops:
  0.6 0.7 copy-start

commit v5 on v4

--- a/solution.py
+++ b/solution.py
@@ -219,11 +219,6 @@
         return part(cp, lax.rem(y + e, Y) * Z + lax.rem(z + d, Z), chunk)
 
     order = [*reversed(ring), 0]
-    for d in order:
-        for e in (2, 1, 3):
-            copy(term(e, d), cy.at[d, e - 1], cy_s, cy_r.at[d], ypeer(e)).start()
-    sent(cp.at[pl.ds(0, (F - Z) * chunk)], cy_s)
-
     arrived(gy.at[pl.ds(0, Y - 1)], gy_r)
     total = gy[0]
     for k in range(1, Y):
@@ -232,6 +227,11 @@
     for d in reversed(ring):
         copy(gz.at[z], gz.at[z], gz_s, gz_r, zpeer(d)).start()
     sent(gz.at[pl.ds(0, Z - 1)], gz_s)
+
+    for d in order:
+        for e in (2, 1, 3):
+            copy(term(e, d), cy.at[d, e - 1], cy_s, cy_r.at[d], ypeer(e)).start()
+    sent(cp.at[pl.ds(0, (F - Z) * chunk)], cy_s)
 
     def combine(d):
         arrived(cy.at[d], cy_r.at[d])

time: 77.2 us -> 77.2 us (level)
  no operation moved by 1% of the time
where the time goes in v5:
time: 77.2 us; the launch traced here: 77 us
  Pallas kernels  73.1 us (95%)
  local copies, waits for them, and re-layouts  3.26 us (4%)
    pallas_call x1, Pallas kernels, local(): pl.pallas_call(exchange, out_shape=(jax.ShapeDtypeStruct((chunk, RANK), F...  73.1 us
    unnamed x5, local copies, waits for them, and re-layouts  3.26 us

profile of v5, /device:TPU:1, one launch (start us, length us, event | category | flops | bytes accessed | tf_op | source)
XLA Modules:
  0.0 77.0 jit_solution(17296332946261935235)
XLA Ops:
  0.6 0.0 copy-start
  0.6 0.7 copy-done
  1.3 73.1 %exchange.1 = (f32[32,128]{1,0:T(8,128)S(1)}, bf16[256,2048]{1,0:T(8,128)(2,1)S(1)}, bf16[256,2048]{1,0:T(8,128)(2,1)S(1)}) custom-call(bf16[256,2048]{1,0:T(8,128)(2,1)} %mom.1, bf16[256,2048]{1,0:T(8,128)(2,1)} %grad.1, f32[32,128]{1,0:T(8,128)S(1)} %copy-done), custom_call_target="tpu_custom_call" | custom-call | tf_op jit(solution)/shard_map/exchange/pallas_call | solution.py:337
  74.4 1.0 %copy.9 = bf16[256,2048]{1,0:T(8,128)(2,1)} copy(bf16[256,2048]{1,0:T(8,128)(2,1)S(1)} %get-tuple-element.12) | data formatting | bytes 2097152
  75.4 1.0 %copy.10 = bf16[256,2048]{1,0:T(8,128)(2,1)} copy(bf16[256,2048]{1,0:T(8,128)(2,1)S(1)} %get-tuple-element.13) | data formatting | bytes 2097152
  76.4 0.6 copy.11
Async XLA Ops:
  0.6 0.7 copy-start
